TPU v7x, 1024 devices: a whole 4x4x32 slice. The times are simulated.
1024 devices in a mesh: blk: 64 (over z, core), sub: 16 (over x, y).
Axes of the slice: x: 4, y: 4, z: 32, core: 2. Of those that a mesh axis runs over, the one named last changes fastest.
Arguments:
- tracer: float32 [4, 28, 131072], P(None, None, ('blk', 'sub')), may hold values from 0 to 2
- edge_flow: float32 [28, 393216], P(None, ('blk', 'sub')), may hold values from -2.7 to 2.7
- edge_owner: int32 [393216], P(('blk', 'sub')), may hold values from 0 to 127
- edge_other: int32 [393216], P(('blk', 'sub')), may hold values from 0 to 255
- stencil: int32 [2, 16, 393216], P(None, None, ('blk', 'sub')), may hold values from 0 to 255
- stencil_coef: float32 [2, 16, 393216], P(None, None, ('blk', 'sub')), may hold values from -6 to 6
- stencil_count: int32 [2, 393216], P(None, ('blk', 'sub')), may hold values from 10 to 16
- send_cells: int32 [8, 16384], P(None, ('blk', 'sub')), may hold values from 0 to 127
- cell_area: float32 [131072], P(('blk', 'sub')), may hold values from 0.5 to 18, as said below
Outputs:
- advected: float32 [4, 28, 131072], P(None, None, ('blk', 'sub'))
- mass_mean: float32 [4, 28], replicated
Inputs may be any that keep to these rules, and one draw needn't show every extreme that they name: `cell_area`: areas of the cells; positive.
All inputs are finite; a program needn't handle non-finite values.
Results may differ from a plain program's by a relative error of at most 0.00018.
Values sent between devices are 32-bit elements; how exact they have to be, the bound alone decides.
No kernel may reach another device: no remote copies, remote signals or barrier semaphores. Data moves between devices by JAX's collectives and lax.ppermute only.
A program may use at most 64 MiB of HBM per device.

v0:
```python
import functools

import jax
import jax.numpy as jnp
from jax import lax
from jax.experimental import pallas as pl
from jax.experimental.pallas import tpu as pltpu
from jax.sharding import PartitionSpec as P

F32 = jnp.float32
BF16 = jnp.bfloat16
PEER = 16
AXES = ("z", "core", "sub")


def split(x):
    hi = x.astype(BF16)
    return hi, (x - hi.astype(F32)).astype(BF16)


def dot(a, b):
    return lax.dot_general(a, b, (((1,), (0,)), ((), ())), preferred_element_type=F32)


def dot_nt(a, b):
    return lax.dot_general(a, b, (((1,), (1,)), ((), ())), preferred_element_type=F32)


def send_lanes(send_ref, wide_ref, backwards):
    groups, peer = send_ref.shape
    wide_ref[...] = jnp.zeros_like(wide_ref)
    wide_ref[:, :peer] = send_ref[...]
    lane = lax.broadcasted_iota(jnp.int32, (groups, 128), 1)
    group = lax.broadcasted_iota(jnp.int32, (groups, 128), 0)
    tiled = jnp.take_along_axis(wide_ref[...], lane % peer, axis=1)
    rows = []
    for back in backwards:
        want = groups - 1 - lane // peer if back else lane // peer
        rows.append(jnp.sum(jnp.where(want == group, tiled, 0), axis=0, keepdims=True))
    return rows


def square(rows):
    return jnp.concatenate([rows, jnp.zeros((128 - rows.shape[0], 128), F32)], axis=0)


def pick(state, lanes):
    return square(jnp.take_along_axis(state, jnp.broadcast_to(lanes, state.shape), axis=1)).T


def put_groups(out, next_ref, prev_ref, up_ref, down_ref):
    next_ref[:48] = jnp.concatenate([out[64:80], out[112:], out[32:48]], axis=0)
    prev_ref[:48] = jnp.concatenate([out[48:64], out[80:96], out[:16]], axis=0)
    up_ref[...] = out[96:112]
    down_ref[...] = out[16:32]


def put_rows(out, up_ref, down_ref, next_ref, prev_ref):
    up_ref[...] = out[80:]
    down_ref[...] = out[:48]
    next_ref[...] = out[64:80]
    prev_ref[...] = out[48:64]


def pack_kernel(tracer, send, stencil, coef, count, owner, other, flow, area,
                next_ref, prev_ref, up_ref, down_ref, lanes_ref, back_ref,
                tracer_ref, stencil_ref, coef_ref, count_ref, owner_ref, other_ref, flow_ref, area_ref,
                send_ref, wide_ref, owner_flat, other_flat, area_flat, sems):
    sources = (tracer, send, owner, other, area, stencil, coef, count, flow)
    targets = (tracer_ref, send_ref, owner_flat, other_flat, area_flat, stencil_ref, coef_ref, count_ref, flow_ref)
    copies = [pltpu.make_async_copy(a, b, sems.at[k]) for k, (a, b) in enumerate(zip(sources, targets))]
    for copy in copies:
        copy.start()
    copies[0].wait()
    copies[1].wait()
    lanes_ref[...], back_ref[...] = send_lanes(send_ref, wide_ref, (False, True))
    put_groups(pick(tracer_ref[...], lanes_ref[...]), next_ref, prev_ref, up_ref, down_ref)
    for copy in copies[2:]:
        copy.wait()
    owner_ref[...] = owner_flat[...].reshape(owner_ref.shape)
    other_ref[...] = other_flat[...].reshape(other_ref.shape)
    area_ref[...] = area_flat[...].reshape(area_ref.shape)


def fill(part, stencil_ref, coef_ref, count_ref, owner_ref, other_ref, mhi_ref, mlo_ref):
    edges = owner_ref.shape[1]
    for chunk in range(edges // 128):
        at = pl.ds(chunk * 128, 128)
        cell = lax.broadcasted_iota(jnp.int32, (128, 128), 0) + part * 128
        curves = []
        for side in range(2):
            total = jnp.zeros((128, 128), F32)
            count = count_ref[pl.ds(side, 1), at]
            for j in range(stencil_ref.shape[1]):
                weight = jnp.where(j < count, coef_ref[side, pl.ds(j, 1), at], 0.0)
                index = stencil_ref[side, pl.ds(j, 1), at]
                total = total + jnp.where(cell == index, weight, 0.0)
            curves.append(total)
        ends = jnp.where(cell == other_ref[:, at], 0.5, 0.0)
        if part == 0:
            ends = ends + jnp.where(cell == owner_ref[:, at], 0.5, 0.0)
        mean = ends - (curves[0] + curves[1]) * (1.0 / 12.0)
        diff = (curves[0] - curves[1]) * (1.0 / 12.0)
        for which, value in enumerate((mean, diff)):
            columns = pl.ds(which * edges + chunk * 128, 128)
            mhi_ref[:, columns], mlo_ref[:, columns] = split(value)


def own_kernel(stencil_ref, coef_ref, count_ref, owner_ref, other_ref, mhi_ref, mlo_ref, div_ref):
    fill(0, stencil_ref, coef_ref, count_ref, owner_ref, other_ref, mhi_ref, mlo_ref)
    cell = lax.broadcasted_iota(jnp.int32, div_ref.shape, 0)
    gain = jnp.where(cell == other_ref[...], 1.0, 0.0) - jnp.where(cell == owner_ref[...], 1.0, 0.0)
    div_ref[...] = gain.astype(BF16)


def halo_kernel(stencil_ref, coef_ref, count_ref, owner_ref, other_ref, flow_ref, ohi_ref, olo_ref,
                mhi_ref, mlo_ref, leak_ref):
    fill(1, stencil_ref, coef_ref, count_ref, owner_ref, other_ref, mhi_ref, mlo_ref)
    edges = owner_ref.shape[1]
    leaves = jnp.where(other_ref[...] < 128, 0.0, -1.0)
    levels = flow_ref.shape[0]
    parts = split(flow_ref[...] * leaves) + split(jnp.abs(flow_ref[...]) * leaves)
    leak_ref[...] = jnp.zeros_like(leak_ref)
    for part, (hi_ref, lo_ref) in enumerate(((ohi_ref, olo_ref), (mhi_ref, mlo_ref))):
        total = jnp.zeros((levels, 128), F32)
        for which in range(2):
            at = pl.ds(which * edges, edges)
            hi, lo = parts[2 * which:2 * which + 2]
            total = total + dot_nt(hi, hi_ref[:, at]) + dot_nt(lo, hi_ref[:, at]) + dot_nt(hi, lo_ref[:, at])
        leak_ref[pl.ds(0, levels), pl.ds(part * 128, 128)] = total


def product(value, mhi_ref, mlo_ref):
    hi, lo = split(value)
    both = dot(jnp.concatenate([hi, lo], axis=0), mhi_ref[...])
    return both[:value.shape[0]] + both[value.shape[0]:] + dot(hi, mlo_ref[...])


def ahead_kernel(state_ref, ohi_ref, olo_ref, picked_ref):
    picked_ref[...] = product(state_ref[...], ohi_ref, olo_ref)


def tendency(halo, picked_ref, mhi_ref, mlo_ref, div_ref, flow_ref, area_ref):
    columns = halo.shape[0]
    edges = div_ref.shape[1]
    picked = picked_ref[...] + product(halo, mhi_ref, mlo_ref)
    flow = flow_ref[...]
    flux = flow * picked[:, :edges] + jnp.abs(flow) * picked[:, edges:]
    both = dot_nt(jnp.concatenate(split(flux), axis=0), div_ref[...])
    return (both[:columns] + both[columns:]) / area_ref[...]


def halo_of(low_ref, high_ref, far_lo_ref, far_hi_ref, columns):
    return jnp.concatenate([far_lo_ref[:48], low_ref[:16], high_ref[:16], far_hi_ref[:48]], axis=0).T[:columns]


def halo_of_rows(far_lo_ref, far_hi_ref, low_ref, high_ref, columns):
    return jnp.concatenate(
        [
            low_ref[16:32], far_lo_ref[16:32], high_ref[16:32], low_ref[:16],
            high_ref[:16], low_ref[32:], far_hi_ref[16:32], high_ref[32:],
        ],
        axis=0,
    ).T[:columns]


def first_kernel(tracer_ref, lanes_ref, leak_ref, h0, h1, h2, h3, m0, m1, m2, m3, m4, m5,
                 new_ref, next_ref, prev_ref, up_ref, down_ref):
    mats = (m0, m1, m2, m3, m4, m5)
    tracer = tracer_ref[...]
    new = tracer + tendency(halo_of(h0, h1, h2, h3, tracer.shape[0]), *mats) / 3.0
    new_ref[...] = new
    put_groups(pick(new, lanes_ref[...]), next_ref, prev_ref, up_ref, down_ref)
    next_ref[48:] = leak_ref[:, 128:]
    prev_ref[48:] = leak_ref[:, 128:]


def second_kernel(levels, tracer_ref, lanes_ref, back_ref, leak_ref, h0, h1, h2, h3, m0, m1, m2, m3, m4, m5,
                  new_ref, up_ref, down_ref, next_ref, prev_ref, mass_ref):
    mats = (m0, m1, m2, m3, m4, m5)
    tracer = tracer_ref[...]
    columns = tracer.shape[0]
    new = tracer + tendency(halo_of(h0, h1, h2, h3, columns), *mats) / 2.0
    new_ref[...] = new
    put_rows(pick(new, lanes_ref[...]), up_ref, down_ref, next_ref, prev_ref)
    label = lax.broadcasted_iota(jnp.int32, (leak_ref.shape[0], 128), 1) // PEER
    shares = jnp.where(label >= 5, h2[48:], h3[48:])
    shares = jnp.where(label == 4, h0[48:], jnp.where(label == 3, h1[48:], shares))
    cell = lax.broadcasted_iota(jnp.int32, (128, 128), 0)
    owner = jnp.where(cell == back_ref[...], 1.0, 0.0).astype(BF16)
    hi, lo = split(shares)
    gain = leak_ref[:, :128] + dot_nt(hi, owner) + dot_nt(lo, owner)
    tracers = columns // levels
    row = lax.broadcasted_iota(jnp.int32, (columns, gain.shape[0]), 0) // tracers
    spread = jnp.where(row == lax.broadcasted_iota(jnp.int32, row.shape, 1), 1.0, 0.0).astype(BF16)
    hi, lo = split(gain)
    area = m5[...]
    weighted = area * tracer + (dot(spread, hi) + dot(spread, lo)) * new
    weighted = jnp.concatenate([weighted, jnp.broadcast_to(area, (128 - columns, 128))], axis=0)
    mass = jnp.sum(weighted.T, axis=0, keepdims=True)
    for device in range(mass_ref.shape[0]):
        mass_ref[device] = jnp.broadcast_to(mass, mass_ref.shape[1:])


def third_kernel(tracer_ref, rows_ref, h0, h1, h2, h3, m0, m1, m2, m3, m4, m5, out_ref, mean_ref):
    mats = (m0, m1, m2, m3, m4, m5)
    out_ref[...] = tracer_ref[...] + tendency(halo_of_rows(h0, h1, h2, h3, tracer_ref.shape[0]), *mats)
    tracers, levels = mean_ref.shape
    total = jnp.sum(rows_ref[...], axis=0)
    mean = jnp.broadcast_to(total / total[:, tracers * levels:tracers * levels + 1], (8, 128))
    lane = lax.broadcasted_iota(jnp.int32, (8, 128), 1) * tracers + lax.broadcasted_iota(jnp.int32, (8, 128), 0)
    mean_ref[...] = jnp.take_along_axis(mean, jnp.minimum(lane, 127), axis=1)[:tracers, :levels]


def relay_kernel(rows_ref, out_ref):
    total = jnp.sum(rows_ref[...], axis=0)[:1]
    for device in range(out_ref.shape[0]):
        out_ref[device] = total


def call(kernel, outs, scratch=(), **more):
    return pl.pallas_call(
        kernel,
        out_shape=outs,
        scratch_shapes=list(scratch),
        compiler_params=pltpu.CompilerParams(vmem_limit_bytes=16 * 2**20),
        **more,
    )


def array(shape, dtype=F32):
    return jax.ShapeDtypeStruct(shape, dtype)


def shift(value, by):
    count = lax.axis_size(AXES)
    return lax.ppermute(value, AXES, [(i, (i + by) % count) for i in range(count)])


def swap(value, first):
    count = lax.axis_size(AXES)
    return lax.ppermute(value, AXES, [(i, (((i - first) % count ^ 1) + first) % count) for i in range(count)])


def hop_along(after, before):
    odd = lax.axis_index("sub") % 2 == 1
    near = swap(jnp.where(odd, before, after), 0)
    far = swap(jnp.where(odd, after, before), 1)
    return jnp.where(odd, near, far), jnp.where(odd, far, near)


def hop_up(low, high, up, down, leak=None):
    width = lax.axis_size("sub")
    up = [low[16:32], up, high[16:32]]
    down = [low[32:48], down, high[32:48]]
    if leak is not None:
        label = lax.broadcasted_iota(jnp.int32, leak.shape, 1) // PEER
        up.append(jnp.where(label == 6, leak, jnp.where(label == 7, low[48:], high[48:])))
        down.append(jnp.where(label == 1, leak, jnp.where(label == 2, low[48:], high[48:])))
    return shift(jnp.concatenate(up, axis=0), width), shift(jnp.concatenate(down, axis=0), -width)


def spread_out(rows, axes, first=0):
    count = lax.axis_size(axes)
    groups = [[(first + i) % count for i in range(count)]] if first else None
    return lax.all_to_all(rows, axes, 0, 0, axis_index_groups=groups, tiled=True)


def body(tracer, edge_flow, edge_owner, edge_other, stencil, stencil_coef, stencil_count, send_cells, cell_area):
    ntracer, nlevel, cells = tracer.shape
    edges = edge_owner.shape[0]
    columns = ntracer * nlevel
    plane, depth = lax.axis_size(("core", "sub")), lax.axis_size("z")
    state = array((columns, cells))

    def messages(extra):
        return [array((48 + extra, 128)), array((48 + extra, 128)), array((PEER, 128)), array((PEER, 128))]

    whole = pl.BlockSpec(memory_space=pltpu.HBM)
    statics = [stencil, stencil_coef, stencil_count, edge_owner, edge_other, edge_flow, cell_area]
    after, before, up, down, lanes, back, rows, *statics, area = call(
        pack_kernel,
        messages(0) + [array((1, cells), jnp.int32)] * 2 + [state]
        + [array(stencil.shape, jnp.int32), array(stencil.shape), array(stencil_count.shape, jnp.int32)]
        + [array((1, edges), jnp.int32)] * 2 + [array(edge_flow.shape), array((1, cells))],
        [pltpu.VMEM(send_cells.shape, jnp.int32), pltpu.VMEM((8, cells), jnp.int32),
         pltpu.VMEM((edges,), jnp.int32), pltpu.VMEM((edges,), jnp.int32), pltpu.VMEM((cells,), F32),
         pltpu.SemaphoreType.DMA((9,))],
        in_specs=[whole] * 9,
    )(*(pltpu.with_memory_space_constraint(x, pltpu.HBM)
        for x in (tracer.transpose(1, 0, 2).reshape(columns, cells), send_cells, *statics)))
    half = [array((cells, 2 * edges), BF16)] * 2

    low, high = hop_along(after, before)
    ohi, olo, divergence = call(own_kernel, half + [array((cells, edges), BF16)])(*statics[:5])
    mhi, mlo, leak = call(halo_kernel, half + [array((32, 2 * cells))])(*statics, ohi, olo)
    low, high, mhi = lax.optimization_barrier((low, high, mhi))
    far_lo, far_hi = hop_up(low, high, up, down)
    flow = jnp.broadcast_to(statics[5][:, None, :], (nlevel, ntracer, edges)).reshape(columns, edges)
    matrices = (mhi, mlo, divergence, flow, area)
    ahead = call(ahead_kernel, array((columns, 2 * edges)))
    one, after, before, up, down = call(first_kernel, [state] + messages(32))(
        rows, lanes, leak, low, high, far_lo, far_hi, ahead(rows, ohi, olo), *matrices)

    low, high = hop_along(after, before)
    far_lo, far_hi = hop_up(low, high, up, down, leak[:, cells:])
    two, up, down, after, before, mass = call(
        functools.partial(second_kernel, nlevel), [state] + messages(0) + [array((plane, 2, 128))]
    )(rows, lanes, back, leak, low, high, far_lo, far_hi, ahead(one, ohi, olo), *matrices)

    width = lax.axis_size("sub")
    far_lo, far_hi = shift(up, width), shift(down, -width)
    mass = spread_out(mass, ("core", "sub"))
    far_lo, far_hi, mass = lax.optimization_barrier((far_lo, far_hi, mass))
    after = jnp.concatenate([after, far_lo[32:], far_hi[32:]], axis=0)
    before = jnp.concatenate([before, far_lo[:16], far_hi[:16]], axis=0)
    odd = lax.axis_index("sub") % 2 == 1
    near = swap(jnp.where(odd, before, after), 0)
    far = swap(jnp.where(odd, after, before), 1)
    mass = call(relay_kernel, array((depth, 1, 128)))(mass)
    mass = spread_out(mass, "z", 3 * depth // 4)
    near, far, mass = lax.optimization_barrier((near, far, mass))
    low, high = jnp.where(odd, near, far), jnp.where(odd, far, near)
    advected, mean = call(third_kernel, [state, array((ntracer, nlevel))])(
        rows, mass, far_lo, far_hi, low, high, ahead(two, ohi, olo), *matrices)
    return advected.reshape(nlevel, ntracer, cells).transpose(1, 0, 2), mean


def solution(mesh):
    blk, sub = mesh.devices.shape
    fine = jax.sharding.Mesh(mesh.devices.reshape(blk // 2, 2, sub), AXES)
    in_specs = (
        P(None, None, AXES), P(None, AXES), P(AXES), P(AXES), P(None, None, AXES),
        P(None, None, AXES), P(None, AXES), P(None, AXES), P(AXES),
    )
    out_specs = (P(None, None, AXES), P())
    return jax.shard_map(body, mesh=fine, in_specs=in_specs, out_specs=out_specs, check_vma=False)
```

profile of v0, /device:TPU:1, one launch (start us, length us, event | category | flops | bytes accessed | tf_op | source)
XLA Modules:
  0.0 92.6 jit_solution(6150052547733659272)
XLA Ops:
  0.6 1.2 %shard_map.104 = (f32[48,128]{1,0:T(8,128)S(1)}, f32[48,128]{1,0:T(8,128)S(1)}, f32[16,128]{1,0:T(8,128)S(1)}, f32[16,128]{1,0:T(8,128)S(1)}, s32[1,128]{1,0:T(1...) custom-call(f32[112,128]{1,0:T(8,128)} %bitcast.6, ...), custom_call_target="tpu_custom_call" | custom-call | tf_op jit(solution)/shard_map/pallas_call | solution.py:281
  1.8 8.2 %collective-permute-start.1 = (f32[48,128]{1,0:T(8,128)S(1)}, f32[48,128]{1,0:T(8,128)S(1)}, u32[]{:S(2)}, u32[]{:S(2)}) collective-permute-start(f32[48,128]{1,0:T(8,128)S(1)} %get-tuple-element.98), channel_id=1, source_target_pairs={{0,1023},{1,2},{2,1},{3,4},{4,3},{5,6},{6,5},{7,8},{8,7},{9,10},{1... | collective-permute-start | bytes 73736 | tf_op jit(solution)/shard_map/ppermute | solution.py:242
  10.1 1.9 %collective-permute-start = (f32[48,128]{1,0:T(8,128)S(1)}, f32[48,128]{1,0:T(8,128)S(1)}, u32[]{:S(2)}, u32[]{:S(2)}) collective-permute-start(f32[48,128]{1,0:T(8,128)S(1)} %get-tuple-element.99), channel_id=1, source_target_pairs={{0,1},{1,0},{2,3},{3,2},{4,5},{5,4},{6,7},{7,6},{8,9},{9,8},{10,11... | collective-permute-start | bytes 73736 | tf_op jit(solution)/shard_map/ppermute | solution.py:242
  12.0 1.0 %shard_map.105 = (bf16[128,768]{1,0:T(8,128)(2,1)S(1)}, bf16[128,768]{1,0:T(8,128)(2,1)S(1)}, bf16[128,384]{1,0:T(8,128)(2,1)S(1)}) custom-call(s32[2,16,384]{2,1,0:T(8,128)S(1)} %get-tuple-element.47.stencil_ref, f32[2,16,384]{2,1,0:T(8,128)S(1)} %get-tuple-element.48.coef_ref, s32[2,384]{1,0:T(2,128)S(1)} %get-tuple-element.49.count_ref, ...), custom_call_target="tpu_custom_call" | custom-call | tf_op jit(solution)/shard_map/pallas_call | solution.py:295
  13.1 1.1 %shard_map.106 = (bf16[128,768]{1,0:T(8,128)(2,1)S(1)}, bf16[128,768]{1,0:T(8,128)(2,1)S(1)}, f32[32,256]{1,0:T(8,128)S(1)}) custom-call(s32[2,16,384]{2,1,0:T(8,128)S(1)} %get-tuple-element.47.stencil_ref, f32[2,16,384]{2,1,0:T(8,128)S(1)} %get-tuple-element.48.coef_ref, s32[2,384]{1,0:T(2,128)S(1)} %get-tuple-element.49.count_ref, ...), custom_call_target="tpu_custom_call" | custom-call | tf_op jit(solution)/shard_map/pallas_call | solution.py:296
  14.2 0.0 collective-permute-done.1
  14.2 0.4 collective-permute-done
  14.7 2.2 %collective-permute-start.2 = (f32[48,128]{1,0:T(8,128)S(1)}, f32[48,128]{1,0:T(8,128)S(1)}, u32[]{:S(2)}, u32[]{:S(2)}) collective-permute-start(f32[48,128]{1,0:T(8,128)S(1)} %pad_maximum_fusion.2), channel_id=1, source_target_pairs={{0,16},{1,17},{2,18},{3,19},{4,20},{5,21},{6,22},{7,23},{8,24},{9,... | collective-permute-start | bytes 73736 | tf_op jit(solution)/shard_map/ppermute | solution.py:237
  16.8 15.1 %collective-permute-start.3 = (f32[48,128]{1,0:T(8,128)S(1)}, f32[48,128]{1,0:T(8,128)S(1)}, u32[]{:S(2)}, u32[]{:S(2)}) collective-permute-start(f32[48,128]{1,0:T(8,128)S(1)} %pad_maximum_fusion.3), channel_id=1, source_target_pairs={{0,1008},{1,1009},{2,1010},{3,1011},{4,1012},{5,1013},{6,1014},{7,... | collective-permute-start | bytes 73736 | tf_op jit(solution)/shard_map/ppermute | solution.py:237
  32.0 0.1 reshape.15.m4
  32.0 0.3 shard_map.107.m0
  32.3 0.3 collective-permute-done.2.h2
  32.6 0.2 collective-permute-done.3.h3
  32.8 0.7 shard_map.108
  33.5 5.7 %collective-permute-start.5 = (f32[80,128]{1,0:T(8,128)S(1)}, f32[80,128]{1,0:T(8,128)S(1)}, u32[]{:S(2)}, u32[]{:S(2)}) collective-permute-start(f32[80,128]{1,0:T(8,128)S(1)} %get-tuple-element.90), channel_id=1, source_target_pairs={{0,1023},{1,2},{2,1},{3,4},{4,3},{5,6},{6,5},{7,8},{8,7},{9,10},{1... | collective-permute-start | bytes 122888 | tf_op jit(solution)/shard_map/ppermute | solution.py:242
  39.2 1.9 %collective-permute-start.4 = (f32[80,128]{1,0:T(8,128)S(1)}, f32[80,128]{1,0:T(8,128)S(1)}, u32[]{:S(2)}, u32[]{:S(2)}) collective-permute-start(f32[80,128]{1,0:T(8,128)S(1)} %get-tuple-element.91), channel_id=1, source_target_pairs={{0,1},{1,0},{2,3},{3,2},{4,5},{5,4},{6,7},{7,6},{8,9},{9,8},{10,11... | collective-permute-start | bytes 122888 | tf_op jit(solution)/shard_map/ppermute | solution.py:242
  41.2 1.0 %collective-permute-done.5 = f32[80,128]{1,0:T(8,128)S(1)} collective-permute-done((f32[80,128]{1,0:T(8,128)S(1)}, f32[80,128]{1,0:T(8,128)S(1)}, u32[]{:S(2)}, u32[]{:S(2)}) %collective-permute-start.5) | collective-permute-done | bytes 40992 | tf_op jit(solution)/shard_map/ppermute | solution.py:242
  42.1 1.8 %collective-permute-done.4 = f32[80,128]{1,0:T(8,128)S(1)} collective-permute-done((f32[80,128]{1,0:T(8,128)S(1)}, f32[80,128]{1,0:T(8,128)S(1)}, u32[]{:S(2)}, u32[]{:S(2)}) %collective-permute-start.4) | collective-permute-done | bytes 40992 | tf_op jit(solution)/shard_map/ppermute | solution.py:242
  44.0 0.0 collective-permute-start.6
  44.1 3.9 %collective-permute-start.7 = (f32[80,128]{1,0:T(8,128)S(1)}, f32[80,128]{1,0:T(8,128)S(1)}, u32[]{:S(2)}, u32[]{:S(2)}) collective-permute-start(f32[80,128]{1,0:T(8,128)S(1)} %pad_maximum_fusion.1), channel_id=1, source_target_pairs={{0,1008},{1,1009},{2,1010},{3,1011},{4,1012},{5,1013},{6,1014},{7,... | collective-permute-start | bytes 122888 | tf_op jit(solution)/shard_map/ppermute | solution.py:237
  48.0 0.3 shard_map.109.m0
  48.3 0.4 collective-permute-done.6.h2
  48.7 0.2 collective-permute-done.7.h3
  48.9 1.3 %shard_map.110 = (f32[112,128]{1,0:T(8,128)S(1)}, f32[48,128]{1,0:T(8,128)S(1)}, f32[48,128]{1,0:T(8,128)S(1)}, f32[16,128]{1,0:T(8,128)S(1)}, f32[16,128]{1,0:T(8,128)S(1)}, /*index=5*/f32[32,2,128]{2,1,0:T(2,128)}) custom-call(f32[112,128]{1,0:T(8,128)S(1)} %get-tuple-element.44.state_ref.tracer_ref, s32[1,128]{1,0:T(1,128)S(1)} %get-tuple-element.45.lanes_ref, ...), custom_call_target="tpu_custom_call" | custom-call | tf_op jit(solution)/shard_map/pallas_call | solution.py:307
  50.2 7.3 %all-to-all-start = ((f32[32,2,128]{2,1,0:T(2,128)}), f32[32,2,128]{2,1,0:T(2,128)S(1)}, u32[]{:S(2)}, u32[]{:S(2)}) async-start(f32[32,2,128]{2,1,0:T(2,128)} %get-tuple-element.75), calls=%async_computation | async-start | bytes 65536 | tf_op jit(solution)/shard_map/all_to_all | solution.py:266
  57.6 0.0 collective-permute-start.8
  57.6 0.5 collective-permute-start.9
  58.1 0.7 collective-permute-done.8.h0
  58.8 2.4 %collective-permute-done.9.h1 = f32[48,128]{1,0:T(8,128)S(1)} collective-permute-done((f32[48,128]{1,0:T(8,128)S(1)}, f32[48,128]{1,0:T(8,128)S(1)}, u32[]{:S(2)}, u32[]{:S(2)}) %collective-permute-start.9) | collective-permute-done | bytes 24608 | tf_op jit(solution)/shard_map/ppermute | solution.py:237
  61.1 3.4 %all-to-all-done.rows_ref = f32[32,2,128]{2,1,0:T(2,128)S(1)} async-done(((f32[32,2,128]{2,1,0:T(2,128)}), f32[32,2,128]{2,1,0:T(2,128)S(1)}, u32[]{:S(2)}, u32[]{:S(2)}) %all-to-all-start) | async-done | bytes 32800 | tf_op jit(solution)/shard_map/all_to_all | solution.py:266
  64.5 0.6 shard_map.111
  65.2 14.9 %all-to-all-start.1 = ((f32[32,1,128]{2,1,0:T(1,128)}), f32[32,1,128]{2,1,0:T(1,128)S(1)}, u32[]{:S(2)}, u32[]{:S(2)}) async-start(f32[32,1,128]{2,1,0:T(1,128)} %shard_map.111), calls=%async_computation.1 | async-start | bytes 32768 | tf_op jit(solution)/shard_map/all_to_all | solution.py:266
  80.1 4.5 %collective-permute-start.11 = (f32[48,128]{1,0:T(8,128)S(1)}, f32[48,128]{1,0:T(8,128)S(1)}, u32[]{:S(2)}, u32[]{:S(2)}) collective-permute-start(f32[48,128]{1,0:T(8,128)S(1)} %get-tuple-element.94), channel_id=1, source_target_pairs={{0,1023},{1,2},{2,1},{3,4},{4,3},{5,6},{6,5},{7,8},{8,7},{9,10},{1... | collective-permute-start | bytes 73736 | tf_op jit(solution)/shard_map/ppermute | solution.py:242
  84.6 1.9 %collective-permute-start.10 = (f32[48,128]{1,0:T(8,128)S(1)}, f32[48,128]{1,0:T(8,128)S(1)}, u32[]{:S(2)}, u32[]{:S(2)}) collective-permute-start(f32[48,128]{1,0:T(8,128)S(1)} %get-tuple-element.95), channel_id=1, source_target_pairs={{0,1},{1,0},{2,3},{3,2},{4,5},{5,4},{6,7},{7,6},{8,9},{9,8},{10,11... | collective-permute-start | bytes 73736 | tf_op jit(solution)/shard_map/ppermute | solution.py:242
  86.6 0.3 shard_map.112.m0
  86.9 2.0 %collective-permute-done.11 = f32[48,128]{1,0:T(8,128)S(1)} collective-permute-done((f32[48,128]{1,0:T(8,128)S(1)}, f32[48,128]{1,0:T(8,128)S(1)}, u32[]{:S(2)}, u32[]{:S(2)}) %collective-permute-start.11) | collective-permute-done | bytes 24608 | tf_op jit(solution)/shard_map/ppermute | solution.py:242
  88.9 0.6 collective-permute-done.10
  89.5 1.9 %all-to-all-done.1.rows_ref = f32[32,1,128]{2,1,0:T(1,128)S(1)} async-done(((f32[32,1,128]{2,1,0:T(1,128)}), f32[32,1,128]{2,1,0:T(1,128)S(1)}, u32[]{:S(2)}, u32[]{:S(2)}) %all-to-all-start.1) | async-done | bytes 16416 | tf_op jit(solution)/shard_map/all_to_all | solution.py:266
  91.4 1.2 %shard_map.113 = (f32[112,128]{1,0:T(8,128)}, f32[4,28]{1,0:T(4,128)}) custom-call(f32[112,128]{1,0:T(8,128)S(1)} %get-tuple-element.44.state_ref.tracer_ref, f32[32,1,128]{2,1,0:T(1,128)S(1)} %all-to-all-done.1.rows_ref, f32[48,128]{1,0:T(8,128)S(1)} %collective-permute-done.8.h0, f32[48,128]{1,0:T(8,128)S(1)} %collective-permute-done.9.h1, ...), custom_call_target="tpu_custom_call" | custom-call | tf_op jit(solution)/shard_map/pallas_call | solution.py:324
  (19 shorter events, 0.1 us)
Async XLA Ops:
  1.8 12.4 %collective-permute-start.1 = (f32[48,128]{1,0:T(8,128)S(1)}, f32[48,128]{1,0:T(8,128)S(1)}, u32[]{:S(2)}, u32[]{:S(2)}) collective-permute-start(f32[48,128]{1,0:T(8,128)S(1)} %get-tuple-element.98), channel_id=1, source_target_pairs={{0,1023},{1,2},{2,1},{3,4},{4,3},{5,6},{6,5},{7,8},{8,7},{9,10},{1... | collective-permute-start | bytes 73736 | tf_op jit(solution)/shard_map/ppermute | solution.py:242
  10.1 4.6 %collective-permute-start = (f32[48,128]{1,0:T(8,128)S(1)}, f32[48,128]{1,0:T(8,128)S(1)}, u32[]{:S(2)}, u32[]{:S(2)}) collective-permute-start(f32[48,128]{1,0:T(8,128)S(1)} %get-tuple-element.99), channel_id=1, source_target_pairs={{0,1},{1,0},{2,3},{3,2},{4,5},{5,4},{6,7},{7,6},{8,9},{9,8},{10,11... | collective-permute-start | bytes 73736 | tf_op jit(solution)/shard_map/ppermute | solution.py:242
  14.7 17.9 %collective-permute-start.2 = (f32[48,128]{1,0:T(8,128)S(1)}, f32[48,128]{1,0:T(8,128)S(1)}, u32[]{:S(2)}, u32[]{:S(2)}) collective-permute-start(f32[48,128]{1,0:T(8,128)S(1)} %pad_maximum_fusion.2), channel_id=1, source_target_pairs={{0,16},{1,17},{2,18},{3,19},{4,20},{5,21},{6,22},{7,23},{8,24},{9,... | collective-permute-start | bytes 73736 | tf_op jit(solution)/shard_map/ppermute | solution.py:237
  16.8 15.9 %collective-permute-start.3 = (f32[48,128]{1,0:T(8,128)S(1)}, f32[48,128]{1,0:T(8,128)S(1)}, u32[]{:S(2)}, u32[]{:S(2)}) collective-permute-start(f32[48,128]{1,0:T(8,128)S(1)} %pad_maximum_fusion.3), channel_id=1, source_target_pairs={{0,1008},{1,1009},{2,1010},{3,1011},{4,1012},{5,1013},{6,1014},{7,... | collective-permute-start | bytes 73736 | tf_op jit(solution)/shard_map/ppermute | solution.py:237
  33.5 8.6 %collective-permute-start.5 = (f32[80,128]{1,0:T(8,128)S(1)}, f32[80,128]{1,0:T(8,128)S(1)}, u32[]{:S(2)}, u32[]{:S(2)}) collective-permute-start(f32[80,128]{1,0:T(8,128)S(1)} %get-tuple-element.90), channel_id=1, source_target_pairs={{0,1023},{1,2},{2,1},{3,4},{4,3},{5,6},{6,5},{7,8},{8,7},{9,10},{1... | collective-permute-start | bytes 122888 | tf_op jit(solution)/shard_map/ppermute | solution.py:242
  39.2 4.7 %collective-permute-start.4 = (f32[80,128]{1,0:T(8,128)S(1)}, f32[80,128]{1,0:T(8,128)S(1)}, u32[]{:S(2)}, u32[]{:S(2)}) collective-permute-start(f32[80,128]{1,0:T(8,128)S(1)} %get-tuple-element.91), channel_id=1, source_target_pairs={{0,1},{1,0},{2,3},{3,2},{4,5},{5,4},{6,7},{7,6},{8,9},{9,8},{10,11... | collective-permute-start | bytes 122888 | tf_op jit(solution)/shard_map/ppermute | solution.py:242
  44.0 4.7 %collective-permute-start.6 = (f32[80,128]{1,0:T(8,128)S(1)}, f32[80,128]{1,0:T(8,128)S(1)}, u32[]{:S(2)}, u32[]{:S(2)}) collective-permute-start(f32[80,128]{1,0:T(8,128)S(1)} %pad_maximum_fusion), channel_id=1, source_target_pairs={{0,16},{1,17},{2,18},{3,19},{4,20},{5,21},{6,22},{7,23},{8,24},{9,... | collective-permute-start | bytes 122888 | tf_op jit(solution)/shard_map/ppermute | solution.py:237
  44.1 4.8 %collective-permute-start.7 = (f32[80,128]{1,0:T(8,128)S(1)}, f32[80,128]{1,0:T(8,128)S(1)}, u32[]{:S(2)}, u32[]{:S(2)}) collective-permute-start(f32[80,128]{1,0:T(8,128)S(1)} %pad_maximum_fusion.1), channel_id=1, source_target_pairs={{0,1008},{1,1009},{2,1010},{3,1011},{4,1012},{5,1013},{6,1014},{7,... | collective-permute-start | bytes 122888 | tf_op jit(solution)/shard_map/ppermute | solution.py:237
  50.2 14.3 %all-to-all-start = ((f32[32,2,128]{2,1,0:T(2,128)}), f32[32,2,128]{2,1,0:T(2,128)S(1)}, u32[]{:S(2)}, u32[]{:S(2)}) async-start(f32[32,2,128]{2,1,0:T(2,128)} %get-tuple-element.75), calls=%async_computation | async-start | bytes 65536 | tf_op jit(solution)/shard_map/all_to_all | solution.py:266
  57.6 1.2 %collective-permute-start.8 = (f32[48,128]{1,0:T(8,128)S(1)}, f32[48,128]{1,0:T(8,128)S(1)}, u32[]{:S(2)}, u32[]{:S(2)}) collective-permute-start(f32[48,128]{1,0:T(8,128)S(1)} %get-tuple-element.73), channel_id=1, source_target_pairs={{0,16},{1,17},{2,18},{3,19},{4,20},{5,21},{6,22},{7,23},{8,24},{9,... | collective-permute-start | bytes 73736 | tf_op jit(solution)/shard_map/ppermute | solution.py:237
  57.6 3.6 %collective-permute-start.9 = (f32[48,128]{1,0:T(8,128)S(1)}, f32[48,128]{1,0:T(8,128)S(1)}, u32[]{:S(2)}, u32[]{:S(2)}) collective-permute-start(f32[48,128]{1,0:T(8,128)S(1)} %get-tuple-element.74), channel_id=1, source_target_pairs={{0,1008},{1,1009},{2,1010},{3,1011},{4,1012},{5,1013},{6,1014},{7,... | collective-permute-start | bytes 73736 | tf_op jit(solution)/shard_map/ppermute | solution.py:237
  65.2 26.2 %all-to-all-start.1 = ((f32[32,1,128]{2,1,0:T(1,128)}), f32[32,1,128]{2,1,0:T(1,128)S(1)}, u32[]{:S(2)}, u32[]{:S(2)}) async-start(f32[32,1,128]{2,1,0:T(1,128)} %shard_map.111), calls=%async_computation.1 | async-start | bytes 32768 | tf_op jit(solution)/shard_map/all_to_all | solution.py:266
  80.1 8.8 %collective-permute-start.11 = (f32[48,128]{1,0:T(8,128)S(1)}, f32[48,128]{1,0:T(8,128)S(1)}, u32[]{:S(2)}, u32[]{:S(2)}) collective-permute-start(f32[48,128]{1,0:T(8,128)S(1)} %get-tuple-element.94), channel_id=1, source_target_pairs={{0,1023},{1,2},{2,1},{3,4},{4,3},{5,6},{6,5},{7,8},{8,7},{9,10},{1... | collective-permute-start | bytes 73736 | tf_op jit(solution)/shard_map/ppermute | solution.py:242
  84.6 4.9 %collective-permute-start.10 = (f32[48,128]{1,0:T(8,128)S(1)}, f32[48,128]{1,0:T(8,128)S(1)}, u32[]{:S(2)}, u32[]{:S(2)}) collective-permute-start(f32[48,128]{1,0:T(8,128)S(1)} %get-tuple-element.95), channel_id=1, source_target_pairs={{0,1},{1,0},{2,3},{3,2},{4,5},{5,4},{6,7},{7,6},{8,9},{9,8},{10,11... | collective-permute-start | bytes 73736 | tf_op jit(solution)/shard_map/ppermute | solution.py:242
where the time goes:
time: 93 us; the launch traced here: 92.6 us
  starting transfers between devices  68.1 us (73%)
  waiting for transfers between devices  15.3 us (16%)
  Pallas kernels  8.12 us (9%)
    ppermute x6, starting transfers between devices, swap(): lax.ppermute(value, AXES, [(i, (((i - first) % count ^ 1) + first) % coun...  24.2 us
    all_to_all x2, starting transfers between devices, spread_out(): lax.all_to_all(rows, axes, 0, 0, axis_index_groups=groups, tiled=True)  22.2 us
    ppermute x6, starting transfers between devices, shift(): lax.ppermute(value, AXES, [(i, (i + by) % count) for i in range(count)])  21.7 us
    ppermute x6, waiting for transfers between devices, swap(): lax.ppermute(value, AXES, [(i, (((i - first) % count ^ 1) + first) % coun...  5.89 us
    all_to_all x2, waiting for transfers between devices, spread_out(): lax.all_to_all(rows, axes, 0, 0, axis_index_groups=groups, tiled=True)  5.28 us
    ppermute x6, waiting for transfers between devices, shift(): lax.ppermute(value, AXES, [(i, (i + by) % count) for i in range(count)])  4.09 us
  transfers between devices with their start and end apart: 14, of which 13 were waited for; matrix products, arithmetic and copies ran while one was open for 0% of the time, Pallas kernels for 3%

commit v1 on v0

--- a/solution.py
+++ b/solution.py
@@ -176,13 +176,12 @@
 
 
 def second_kernel(levels, tracer_ref, lanes_ref, back_ref, leak_ref, h0, h1, h2, h3, m0, m1, m2, m3, m4, m5,
-                  new_ref, up_ref, down_ref, next_ref, prev_ref, mass_ref):
+                  new_ref, up_ref, down_ref, next_ref, prev_ref, mass_ref, mass_rows, sem):
     mats = (m0, m1, m2, m3, m4, m5)
     tracer = tracer_ref[...]
     columns = tracer.shape[0]
     new = tracer + tendency(halo_of(h0, h1, h2, h3, columns), *mats) / 2.0
     new_ref[...] = new
-    put_rows(pick(new, lanes_ref[...]), up_ref, down_ref, next_ref, prev_ref)
     label = lax.broadcasted_iota(jnp.int32, (leak_ref.shape[0], 128), 1) // PEER
     shares = jnp.where(label >= 5, h2[48:], h3[48:])
     shares = jnp.where(label == 4, h0[48:], jnp.where(label == 3, h1[48:], shares))
@@ -198,18 +197,25 @@
     weighted = area * tracer + (dot(spread, hi) + dot(spread, lo)) * new
     weighted = jnp.concatenate([weighted, jnp.broadcast_to(area, (128 - columns, 128))], axis=0)
     mass = jnp.sum(weighted.T, axis=0, keepdims=True)
-    for device in range(mass_ref.shape[0]):
-        mass_ref[device] = jnp.broadcast_to(mass, mass_ref.shape[1:])
-
-
-def third_kernel(tracer_ref, rows_ref, h0, h1, h2, h3, m0, m1, m2, m3, m4, m5, out_ref, mean_ref):
+    for device in range(mass_rows.shape[0]):
+        mass_rows[device] = jnp.broadcast_to(mass, mass_rows.shape[1:])
+    copy = pltpu.make_async_copy(mass_rows, mass_ref, sem)
+    copy.start()
+    put_rows(pick(new, lanes_ref[...]), up_ref, down_ref, next_ref, prev_ref)
+    copy.wait()
+
+
+def third_kernel(tracer_ref, rows_ref, h0, h1, h2, h3, m0, m1, m2, m3, m4, m5, out_ref, mean_ref, rows_out, sem):
     mats = (m0, m1, m2, m3, m4, m5)
-    out_ref[...] = tracer_ref[...] + tendency(halo_of_rows(h0, h1, h2, h3, tracer_ref.shape[0]), *mats)
+    rows_out[...] = tracer_ref[...] + tendency(halo_of_rows(h0, h1, h2, h3, tracer_ref.shape[0]), *mats)
+    copy = pltpu.make_async_copy(rows_out, out_ref, sem)
+    copy.start()
     tracers, levels = mean_ref.shape
     total = jnp.sum(rows_ref[...], axis=0)
     mean = jnp.broadcast_to(total / total[:, tracers * levels:tracers * levels + 1], (8, 128))
     lane = lax.broadcasted_iota(jnp.int32, (8, 128), 1) * tracers + lax.broadcasted_iota(jnp.int32, (8, 128), 0)
     mean_ref[...] = jnp.take_along_axis(mean, jnp.minimum(lane, 127), axis=1)[:tracers, :levels]
+    copy.wait()
 
 
 def relay_kernel(rows_ref, out_ref):
@@ -305,7 +311,9 @@
     low, high = hop_along(after, before)
     far_lo, far_hi = hop_up(low, high, up, down, leak[:, cells:])
     two, up, down, after, before, mass = call(
-        functools.partial(second_kernel, nlevel), [state] + messages(0) + [array((plane, 2, 128))]
+        functools.partial(second_kernel, nlevel), [state] + messages(0) + [array((plane, 2, 128))],
+        [pltpu.VMEM((plane, 2, 128), F32), pltpu.SemaphoreType.DMA],
+        out_specs=[pl.BlockSpec(memory_space=pltpu.VMEM)] * 5 + [pl.BlockSpec(memory_space=pltpu.HBM)],
     )(rows, lanes, back, leak, low, high, far_lo, far_hi, ahead(one, ohi, olo), *matrices)
 
     width = lax.axis_size("sub")
@@ -321,7 +329,10 @@
     mass = spread_out(mass, "z", 3 * depth // 4)
     near, far, mass = lax.optimization_barrier((near, far, mass))
     low, high = jnp.where(odd, near, far), jnp.where(odd, far, near)
-    advected, mean = call(third_kernel, [state, array((ntracer, nlevel))])(
+    advected, mean = call(
+        third_kernel, [state, array((ntracer, nlevel))], [pltpu.VMEM((columns, cells), F32), pltpu.SemaphoreType.DMA],
+        out_specs=[pl.BlockSpec(memory_space=pltpu.HBM), pl.BlockSpec(memory_space=pltpu.VMEM)],
+    )(
         rows, mass, far_lo, far_hi, low, high, ahead(two, ohi, olo), *matrices)
     return advected.reshape(nlevel, ntracer, cells).transpose(1, 0, 2), mean
 

time: 93 us -> 93.6 us (level)
  no operation moved by 1% of the time
where the time goes in v1:
time: 93.6 us; the launch traced here: 93.2 us
  starting transfers between devices  68.2 us (73%)
  waiting for transfers between devices  15.3 us (16%)
  Pallas kernels  8.72 us (9%)
    ppermute x6, starting transfers between devices, swap(): lax.ppermute(value, AXES, [(i, (((i - first) % count ^ 1) + first) % coun...  24.2 us
    all_to_all x2, starting transfers between devices, spread_out(): lax.all_to_all(rows, axes, 0, 0, axis_index_groups=groups, tiled=True)  22.2 us
    ppermute x6, starting transfers between devices, shift(): lax.ppermute(value, AXES, [(i, (i + by) % count) for i in range(count)])  21.7 us
    ppermute x6, waiting for transfers between devices, swap(): lax.ppermute(value, AXES, [(i, (((i - first) % count ^ 1) + first) % coun...  5.88 us
    all_to_all x2, waiting for transfers between devices, spread_out(): lax.all_to_all(rows, axes, 0, 0, axis_index_groups=groups, tiled=True)  5.28 us
    ppermute x6, waiting for transfers between devices, shift(): lax.ppermute(value, AXES, [(i, (i + by) % count) for i in range(count)])  4.09 us
  transfers between devices with their start and end apart: 14, of which 13 were waited for; matrix products, arithmetic and copies ran while one was open for 0% of the time, Pallas kernels for 3%

profile of v1, /device:TPU:1, one launch (start us, length us, event | category | flops | bytes accessed | tf_op | source)
XLA Modules:
  0.0 93.2 jit_solution(9078017600923351793)
XLA Ops:
  0.6 1.2 %shard_map.104 = (f32[48,128]{1,0:T(8,128)S(1)}, f32[48,128]{1,0:T(8,128)S(1)}, f32[16,128]{1,0:T(8,128)S(1)}, f32[16,128]{1,0:T(8,128)S(1)}, s32[1,128]{1,0:T(1...) custom-call(f32[112,128]{1,0:T(8,128)} %bitcast.6, ...), custom_call_target="tpu_custom_call" | custom-call | tf_op jit(solution)/shard_map/pallas_call | solution.py:287
  1.8 8.2 %collective-permute-start.1 = (f32[48,128]{1,0:T(8,128)S(1)}, f32[48,128]{1,0:T(8,128)S(1)}, u32[]{:S(2)}, u32[]{:S(2)}) collective-permute-start(f32[48,128]{1,0:T(8,128)S(1)} %get-tuple-element.98), channel_id=1, source_target_pairs={{0,1023},{1,2},{2,1},{3,4},{4,3},{5,6},{6,5},{7,8},{8,7},{9,10},{1... | collective-permute-start | bytes 73736 | tf_op jit(solution)/shard_map/ppermute | solution.py:248
  10.1 1.9 %collective-permute-start = (f32[48,128]{1,0:T(8,128)S(1)}, f32[48,128]{1,0:T(8,128)S(1)}, u32[]{:S(2)}, u32[]{:S(2)}) collective-permute-start(f32[48,128]{1,0:T(8,128)S(1)} %get-tuple-element.99), channel_id=1, source_target_pairs={{0,1},{1,0},{2,3},{3,2},{4,5},{5,4},{6,7},{7,6},{8,9},{9,8},{10,11... | collective-permute-start | bytes 73736 | tf_op jit(solution)/shard_map/ppermute | solution.py:248
  12.0 1.0 %shard_map.105 = (bf16[128,768]{1,0:T(8,128)(2,1)S(1)}, bf16[128,768]{1,0:T(8,128)(2,1)S(1)}, bf16[128,384]{1,0:T(8,128)(2,1)S(1)}) custom-call(s32[2,16,384]{2,1,0:T(8,128)S(1)} %get-tuple-element.47.stencil_ref, f32[2,16,384]{2,1,0:T(8,128)S(1)} %get-tuple-element.48.coef_ref, s32[2,384]{1,0:T(2,128)S(1)} %get-tuple-element.49.count_ref, ...), custom_call_target="tpu_custom_call" | custom-call | tf_op jit(solution)/shard_map/pallas_call | solution.py:301
  13.1 1.1 %shard_map.106 = (bf16[128,768]{1,0:T(8,128)(2,1)S(1)}, bf16[128,768]{1,0:T(8,128)(2,1)S(1)}, f32[32,256]{1,0:T(8,128)S(1)}) custom-call(s32[2,16,384]{2,1,0:T(8,128)S(1)} %get-tuple-element.47.stencil_ref, f32[2,16,384]{2,1,0:T(8,128)S(1)} %get-tuple-element.48.coef_ref, s32[2,384]{1,0:T(2,128)S(1)} %get-tuple-element.49.count_ref, ...), custom_call_target="tpu_custom_call" | custom-call | tf_op jit(solution)/shard_map/pallas_call | solution.py:302
  14.2 0.0 collective-permute-done.1
  14.2 0.4 collective-permute-done
  14.7 2.2 %collective-permute-start.2 = (f32[48,128]{1,0:T(8,128)S(1)}, f32[48,128]{1,0:T(8,128)S(1)}, u32[]{:S(2)}, u32[]{:S(2)}) collective-permute-start(f32[48,128]{1,0:T(8,128)S(1)} %pad_maximum_fusion.2), channel_id=1, source_target_pairs={{0,16},{1,17},{2,18},{3,19},{4,20},{5,21},{6,22},{7,23},{8,24},{9,... | collective-permute-start | bytes 73736 | tf_op jit(solution)/shard_map/ppermute | solution.py:243
  16.8 15.1 %collective-permute-start.3 = (f32[48,128]{1,0:T(8,128)S(1)}, f32[48,128]{1,0:T(8,128)S(1)}, u32[]{:S(2)}, u32[]{:S(2)}) collective-permute-start(f32[48,128]{1,0:T(8,128)S(1)} %pad_maximum_fusion.3), channel_id=1, source_target_pairs={{0,1008},{1,1009},{2,1010},{3,1011},{4,1012},{5,1013},{6,1014},{7,... | collective-permute-start | bytes 73736 | tf_op jit(solution)/shard_map/ppermute | solution.py:243
  32.0 0.1 reshape.15.m4
  32.0 0.3 shard_map.107.m0
  32.3 0.3 collective-permute-done.2.h2
  32.6 0.2 collective-permute-done.3.h3
  32.8 0.7 shard_map.108
  33.5 5.7 %collective-permute-start.5 = (f32[80,128]{1,0:T(8,128)S(1)}, f32[80,128]{1,0:T(8,128)S(1)}, u32[]{:S(2)}, u32[]{:S(2)}) collective-permute-start(f32[80,128]{1,0:T(8,128)S(1)} %get-tuple-element.90), channel_id=1, source_target_pairs={{0,1023},{1,2},{2,1},{3,4},{4,3},{5,6},{6,5},{7,8},{8,7},{9,10},{1... | collective-permute-start | bytes 122888 | tf_op jit(solution)/shard_map/ppermute | solution.py:248
  39.2 1.9 %collective-permute-start.4 = (f32[80,128]{1,0:T(8,128)S(1)}, f32[80,128]{1,0:T(8,128)S(1)}, u32[]{:S(2)}, u32[]{:S(2)}) collective-permute-start(f32[80,128]{1,0:T(8,128)S(1)} %get-tuple-element.91), channel_id=1, source_target_pairs={{0,1},{1,0},{2,3},{3,2},{4,5},{5,4},{6,7},{7,6},{8,9},{9,8},{10,11... | collective-permute-start | bytes 122888 | tf_op jit(solution)/shard_map/ppermute | solution.py:248
  41.2 1.0 %collective-permute-done.5 = f32[80,128]{1,0:T(8,128)S(1)} collective-permute-done((f32[80,128]{1,0:T(8,128)S(1)}, f32[80,128]{1,0:T(8,128)S(1)}, u32[]{:S(2)}, u32[]{:S(2)}) %collective-permute-start.5) | collective-permute-done | bytes 40992 | tf_op jit(solution)/shard_map/ppermute | solution.py:248
  42.1 1.8 %collective-permute-done.4 = f32[80,128]{1,0:T(8,128)S(1)} collective-permute-done((f32[80,128]{1,0:T(8,128)S(1)}, f32[80,128]{1,0:T(8,128)S(1)}, u32[]{:S(2)}, u32[]{:S(2)}) %collective-permute-start.4) | collective-permute-done | bytes 40992 | tf_op jit(solution)/shard_map/ppermute | solution.py:248
  44.0 0.0 collective-permute-start.6
  44.1 3.9 %collective-permute-start.7 = (f32[80,128]{1,0:T(8,128)S(1)}, f32[80,128]{1,0:T(8,128)S(1)}, u32[]{:S(2)}, u32[]{:S(2)}) collective-permute-start(f32[80,128]{1,0:T(8,128)S(1)} %pad_maximum_fusion.1), channel_id=1, source_target_pairs={{0,1008},{1,1009},{2,1010},{3,1011},{4,1012},{5,1013},{6,1014},{7,... | collective-permute-start | bytes 122888 | tf_op jit(solution)/shard_map/ppermute | solution.py:243
  48.0 0.3 shard_map.109.m0
  48.3 0.4 collective-permute-done.6.h2
  48.7 0.2 collective-permute-done.7.h3
  48.9 1.3 %shard_map.110 = (f32[112,128]{1,0:T(8,128)S(1)}, f32[48,128]{1,0:T(8,128)S(1)}, f32[48,128]{1,0:T(8,128)S(1)}, f32[16,128]{1,0:T(8,128)S(1)}, f32[16,128]{1,0:T(8,128)S(1)}, /*index=5*/f32[32,2,128]{2,1,0:T(2,128)}) custom-call(f32[112,128]{1,0:T(8,128)S(1)} %get-tuple-element.44.state_ref.tracer_ref, s32[1,128]{1,0:T(1,128)S(1)} %get-tuple-element.45.lanes_ref, ...), custom_call_target="tpu_custom_call" | custom-call | tf_op jit(solution)/shard_map/pallas_call | solution.py:313
  50.2 7.4 %all-to-all-start = ((f32[32,2,128]{2,1,0:T(2,128)}), f32[32,2,128]{2,1,0:T(2,128)S(1)}, u32[]{:S(2)}, u32[]{:S(2)}) async-start(f32[32,2,128]{2,1,0:T(2,128)} %get-tuple-element.75), calls=%async_computation | async-start | bytes 65536 | tf_op jit(solution)/shard_map/all_to_all | solution.py:272
  57.6 0.0 collective-permute-start.8
  57.6 0.5 collective-permute-start.9
  58.1 0.7 collective-permute-done.8.h0
  58.8 2.4 %collective-permute-done.9.h1 = f32[48,128]{1,0:T(8,128)S(1)} collective-permute-done((f32[48,128]{1,0:T(8,128)S(1)}, f32[48,128]{1,0:T(8,128)S(1)}, u32[]{:S(2)}, u32[]{:S(2)}) %collective-permute-start.9) | collective-permute-done | bytes 24608 | tf_op jit(solution)/shard_map/ppermute | solution.py:243
  61.2 3.4 %all-to-all-done.rows_ref = f32[32,2,128]{2,1,0:T(2,128)S(1)} async-done(((f32[32,2,128]{2,1,0:T(2,128)}), f32[32,2,128]{2,1,0:T(2,128)S(1)}, u32[]{:S(2)}, u32[]{:S(2)}) %all-to-all-start) | async-done | bytes 32800 | tf_op jit(solution)/shard_map/all_to_all | solution.py:272
  64.6 0.6 shard_map.111
  65.2 14.9 %all-to-all-start.1 = ((f32[32,1,128]{2,1,0:T(1,128)}), f32[32,1,128]{2,1,0:T(1,128)S(1)}, u32[]{:S(2)}, u32[]{:S(2)}) async-start(f32[32,1,128]{2,1,0:T(1,128)} %shard_map.111), calls=%async_computation.1 | async-start | bytes 32768 | tf_op jit(solution)/shard_map/all_to_all | solution.py:272
  80.1 4.5 %collective-permute-start.11 = (f32[48,128]{1,0:T(8,128)S(1)}, f32[48,128]{1,0:T(8,128)S(1)}, u32[]{:S(2)}, u32[]{:S(2)}) collective-permute-start(f32[48,128]{1,0:T(8,128)S(1)} %get-tuple-element.94), channel_id=1, source_target_pairs={{0,1023},{1,2},{2,1},{3,4},{4,3},{5,6},{6,5},{7,8},{8,7},{9,10},{1... | collective-permute-start | bytes 73736 | tf_op jit(solution)/shard_map/ppermute | solution.py:248
  84.7 1.9 %collective-permute-start.10 = (f32[48,128]{1,0:T(8,128)S(1)}, f32[48,128]{1,0:T(8,128)S(1)}, u32[]{:S(2)}, u32[]{:S(2)}) collective-permute-start(f32[48,128]{1,0:T(8,128)S(1)} %get-tuple-element.95), channel_id=1, source_target_pairs={{0,1},{1,0},{2,3},{3,2},{4,5},{5,4},{6,7},{7,6},{8,9},{9,8},{10,11... | collective-permute-start | bytes 73736 | tf_op jit(solution)/shard_map/ppermute | solution.py:248
  86.6 0.3 shard_map.112.m0
  86.9 2.0 %collective-permute-done.11 = f32[48,128]{1,0:T(8,128)S(1)} collective-permute-done((f32[48,128]{1,0:T(8,128)S(1)}, f32[48,128]{1,0:T(8,128)S(1)}, u32[]{:S(2)}, u32[]{:S(2)}) %collective-permute-start.11) | collective-permute-done | bytes 24608 | tf_op jit(solution)/shard_map/ppermute | solution.py:248
  88.9 0.6 collective-permute-done.10
  89.5 1.9 %all-to-all-done.1.rows_ref = f32[32,1,128]{2,1,0:T(1,128)S(1)} async-done(((f32[32,1,128]{2,1,0:T(1,128)}), f32[32,1,128]{2,1,0:T(1,128)S(1)}, u32[]{:S(2)}, u32[]{:S(2)}) %all-to-all-start.1) | async-done | bytes 16416 | tf_op jit(solution)/shard_map/all_to_all | solution.py:272
  91.4 1.8 %shard_map.113 = (f32[112,128]{1,0:T(8,128)}, f32[4,28]{1,0:T(4,128)}) custom-call(f32[112,128]{1,0:T(8,128)S(1)} %get-tuple-element.44.state_ref.tracer_ref, f32[32,1,128]{2,1,0:T(1,128)S(1)} %all-to-all-done.1.rows_ref, f32[48,128]{1,0:T(8,128)S(1)} %collective-permute-done.8.h0, f32[48,128]{1,0:T(8,128)S(1)} %collective-permute-done.9.h1, ...), custom_call_target="tpu_custom_call" | custom-call | tf_op jit(solution)/shard_map/pallas_call | solution.py:332
  (19 shorter events, 0.1 us)
Async XLA Ops:
  1.8 12.4 %collective-permute-start.1 = (f32[48,128]{1,0:T(8,128)S(1)}, f32[48,128]{1,0:T(8,128)S(1)}, u32[]{:S(2)}, u32[]{:S(2)}) collective-permute-start(f32[48,128]{1,0:T(8,128)S(1)} %get-tuple-element.98), channel_id=1, source_target_pairs={{0,1023},{1,2},{2,1},{3,4},{4,3},{5,6},{6,5},{7,8},{8,7},{9,10},{1... | collective-permute-start | bytes 73736 | tf_op jit(solution)/shard_map/ppermute | solution.py:248
  10.1 4.6 %collective-permute-start = (f32[48,128]{1,0:T(8,128)S(1)}, f32[48,128]{1,0:T(8,128)S(1)}, u32[]{:S(2)}, u32[]{:S(2)}) collective-permute-start(f32[48,128]{1,0:T(8,128)S(1)} %get-tuple-element.99), channel_id=1, source_target_pairs={{0,1},{1,0},{2,3},{3,2},{4,5},{5,4},{6,7},{7,6},{8,9},{9,8},{10,11... | collective-permute-start | bytes 73736 | tf_op jit(solution)/shard_map/ppermute | solution.py:248
  14.7 17.9 %collective-permute-start.2 = (f32[48,128]{1,0:T(8,128)S(1)}, f32[48,128]{1,0:T(8,128)S(1)}, u32[]{:S(2)}, u32[]{:S(2)}) collective-permute-start(f32[48,128]{1,0:T(8,128)S(1)} %pad_maximum_fusion.2), channel_id=1, source_target_pairs={{0,16},{1,17},{2,18},{3,19},{4,20},{5,21},{6,22},{7,23},{8,24},{9,... | collective-permute-start | bytes 73736 | tf_op jit(solution)/shard_map/ppermute | solution.py:243
  16.8 15.9 %collective-permute-start.3 = (f32[48,128]{1,0:T(8,128)S(1)}, f32[48,128]{1,0:T(8,128)S(1)}, u32[]{:S(2)}, u32[]{:S(2)}) collective-permute-start(f32[48,128]{1,0:T(8,128)S(1)} %pad_maximum_fusion.3), channel_id=1, source_target_pairs={{0,1008},{1,1009},{2,1010},{3,1011},{4,1012},{5,1013},{6,1014},{7,... | collective-permute-start | bytes 73736 | tf_op jit(solution)/shard_map/ppermute | solution.py:243
  33.5 8.6 %collective-permute-start.5 = (f32[80,128]{1,0:T(8,128)S(1)}, f32[80,128]{1,0:T(8,128)S(1)}, u32[]{:S(2)}, u32[]{:S(2)}) collective-permute-start(f32[80,128]{1,0:T(8,128)S(1)} %get-tuple-element.90), channel_id=1, source_target_pairs={{0,1023},{1,2},{2,1},{3,4},{4,3},{5,6},{6,5},{7,8},{8,7},{9,10},{1... | collective-permute-start | bytes 122888 | tf_op jit(solution)/shard_map/ppermute | solution.py:248
  39.2 4.7 %collective-permute-start.4 = (f32[80,128]{1,0:T(8,128)S(1)}, f32[80,128]{1,0:T(8,128)S(1)}, u32[]{:S(2)}, u32[]{:S(2)}) collective-permute-start(f32[80,128]{1,0:T(8,128)S(1)} %get-tuple-element.91), channel_id=1, source_target_pairs={{0,1},{1,0},{2,3},{3,2},{4,5},{5,4},{6,7},{7,6},{8,9},{9,8},{10,11... | collective-permute-start | bytes 122888 | tf_op jit(solution)/shard_map/ppermute | solution.py:248
  44.0 4.7 %collective-permute-start.6 = (f32[80,128]{1,0:T(8,128)S(1)}, f32[80,128]{1,0:T(8,128)S(1)}, u32[]{:S(2)}, u32[]{:S(2)}) collective-permute-start(f32[80,128]{1,0:T(8,128)S(1)} %pad_maximum_fusion), channel_id=1, source_target_pairs={{0,16},{1,17},{2,18},{3,19},{4,20},{5,21},{6,22},{7,23},{8,24},{9,... | collective-permute-start | bytes 122888 | tf_op jit(solution)/shard_map/ppermute | solution.py:243
  44.1 4.8 %collective-permute-start.7 = (f32[80,128]{1,0:T(8,128)S(1)}, f32[80,128]{1,0:T(8,128)S(1)}, u32[]{:S(2)}, u32[]{:S(2)}) collective-permute-start(f32[80,128]{1,0:T(8,128)S(1)} %pad_maximum_fusion.1), channel_id=1, source_target_pairs={{0,1008},{1,1009},{2,1010},{3,1011},{4,1012},{5,1013},{6,1014},{7,... | collective-permute-start | bytes 122888 | tf_op jit(solution)/shard_map/ppermute | solution.py:243
  50.2 14.3 %all-to-all-start = ((f32[32,2,128]{2,1,0:T(2,128)}), f32[32,2,128]{2,1,0:T(2,128)S(1)}, u32[]{:S(2)}, u32[]{:S(2)}) async-start(f32[32,2,128]{2,1,0:T(2,128)} %get-tuple-element.75), calls=%async_computation | async-start | bytes 65536 | tf_op jit(solution)/shard_map/all_to_all | solution.py:272
  57.6 1.2 %collective-permute-start.8 = (f32[48,128]{1,0:T(8,128)S(1)}, f32[48,128]{1,0:T(8,128)S(1)}, u32[]{:S(2)}, u32[]{:S(2)}) collective-permute-start(f32[48,128]{1,0:T(8,128)S(1)} %get-tuple-element.73), channel_id=1, source_target_pairs={{0,16},{1,17},{2,18},{3,19},{4,20},{5,21},{6,22},{7,23},{8,24},{9,... | collective-permute-start | bytes 73736 | tf_op jit(solution)/shard_map/ppermute | solution.py:243
  57.6 3.6 %collective-permute-start.9 = (f32[48,128]{1,0:T(8,128)S(1)}, f32[48,128]{1,0:T(8,128)S(1)}, u32[]{:S(2)}, u32[]{:S(2)}) collective-permute-start(f32[48,128]{1,0:T(8,128)S(1)} %get-tuple-element.74), channel_id=1, source_target_pairs={{0,1008},{1,1009},{2,1010},{3,1011},{4,1012},{5,1013},{6,1014},{7,... | collective-permute-start | bytes 73736 | tf_op jit(solution)/shard_map/ppermute | solution.py:243
  65.2 26.2 %all-to-all-start.1 = ((f32[32,1,128]{2,1,0:T(1,128)}), f32[32,1,128]{2,1,0:T(1,128)S(1)}, u32[]{:S(2)}, u32[]{:S(2)}) async-start(f32[32,1,128]{2,1,0:T(1,128)} %shard_map.111), calls=%async_computation.1 | async-start | bytes 32768 | tf_op jit(solution)/shard_map/all_to_all | solution.py:272
  80.1 8.8 %collective-permute-start.11 = (f32[48,128]{1,0:T(8,128)S(1)}, f32[48,128]{1,0:T(8,128)S(1)}, u32[]{:S(2)}, u32[]{:S(2)}) collective-permute-start(f32[48,128]{1,0:T(8,128)S(1)} %get-tuple-element.94), channel_id=1, source_target_pairs={{0,1023},{1,2},{2,1},{3,4},{4,3},{5,6},{6,5},{7,8},{8,7},{9,10},{1... | collective-permute-start | bytes 73736 | tf_op jit(solution)/shard_map/ppermute | solution.py:248
  84.7 4.9 %collective-permute-start.10 = (f32[48,128]{1,0:T(8,128)S(1)}, f32[48,128]{1,0:T(8,128)S(1)}, u32[]{:S(2)}, u32[]{:S(2)}) collective-permute-start(f32[48,128]{1,0:T(8,128)S(1)} %get-tuple-element.95), channel_id=1, source_target_pairs={{0,1},{1,0},{2,3},{3,2},{4,5},{5,4},{6,7},{7,6},{8,9},{9,8},{10,11... | collective-permute-start | bytes 73736 | tf_op jit(solution)/shard_map/ppermute | solution.py:248
